TPU v7x, 256 devices: a whole 4x4x8 slice. The times are simulated.
256 devices in a mesh: seq: 128 (over y_hi, z, x, core), ch: 2 (over y_lo).
Axes of the slice: x: 4, y: 4 (y_hi: 2, y_lo: 2; y = y_hi * 2 + y_lo), z: 8, core: 2. Of those that a mesh axis runs over, the one named last changes fastest.
Arguments:
- seq_in: bfloat16 [65536, 1536], P('seq', 'ch'), may hold values from -6 to 6
- gate_in: bfloat16 [65536, 1536], P('seq', 'ch'), may hold values from -6 to 6
- first_blocks: bfloat16 [128, 512, 512], P('seq'), may hold values from -0.25 to 0.25
- second_blocks: bfloat16 [512, 128, 128], P('seq'), may hold values from -0.5 to 0.5
- out_weight: bfloat16 [1536, 1536], P(None, 'ch'), may hold values from -0.15625 to 0.15625
- cotangent: bfloat16 [65536, 1536], P('seq', 'ch'), may hold values from -6 to 6
Outputs:
- result: bfloat16 [65536, 1536], P('seq', 'ch')
- grad_in: bfloat16 [65536, 1536], P('seq', 'ch')
All inputs are finite; a program needn't handle non-finite values.
Results may differ from a plain program's by a relative error of at most 0.018.
Values may be sent and summed in bfloat16 or wider, within the bound.
A program may use at most 64 MiB of HBM per device.

v0:
```python
import jax
import jax.numpy as jnp
from jax import lax
from jax.experimental import pallas as pl
from jax.experimental.pallas import tpu as pltpu
from jax.sharding import PartitionSpec as P

MESH = pl.DeviceIdType.MESH
SEQ = 128
CHIPS = SEQ // 2
ROWS = 8
BLOCK = 512
WIDTH = 768
HALF = WIDTH // 2
COLS = HALF // 128
F32 = jnp.float32
BF16 = jnp.bfloat16


def dot(a, b, ca=1, cb=0):
    return lax.dot_general(a, b, (((ca,), (cb,)), ((), ())), preferred_element_type=F32)


def kernel(
    seq_hbm, gate_hbm, first_hbm, second_hbm, weight_hbm, cot_hbm,
    result_ref, grad_ref,
    seq, gate_in, blocks, second, weight, cot,
    gate, own_part, part_send, part_recv,
    a_send, a_recv, m_send, a_ret,
    b_send, b_recv, g_send, b_ret,
    wide, wide_out, gated, gated_other, total,
    load_sem, second_sem, part_sem, gated_sem, send_sem, recv_sem, a_ret_sem, b_ret_sem,
):
    me = lax.axis_index("seq")
    ch = lax.axis_index("ch")
    chip, core = me // 2, lax.rem(me, 2)
    partner = me + 1 - 2 * core
    across = {"ch": 1 - ch}
    hub = core * CHIPS + chip

    loads = [
        pltpu.make_async_copy(src, dst, load_sem.at[k])
        for k, (src, dst) in enumerate(
            [
                (first_hbm, blocks),
                (seq_hbm, seq),
                (cot_hbm, cot),
                (weight_hbm, weight),
                (gate_hbm, gate_in),
                (second_hbm, second.at[pl.ds(core * 4, 4)]),
            ]
        )
    ]
    for load in loads:
        load.start()

    barrier = pltpu.get_barrier_semaphore()

    @pl.loop(1, SEQ)
    def _(s):
        pl.semaphore_signal(
            barrier, inc=1, device_id={"seq": lax.rem(me + s, SEQ)}, device_id_type=MESH
        )

    pl.semaphore_signal(barrier, inc=1, device_id=across, device_id_type=MESH)

    def columns(j):
        return pl.ds(j * HALF, HALF)

    def slots(j):
        return pl.ds(j * CHIPS, CHIPS)

    loads[0].wait()
    loads[1].wait()
    for j in range(2):
        part = dot(blocks[0], seq[:, columns(j)])
        a_send[slots(j)] = part.reshape(CHIPS, ROWS, HALF).astype(BF16)
    loads[2].wait()
    loads[3].wait()
    for j in range(2):
        rows = weight[pl.ds(pl.multiple_of((1 - ch) * WIDTH + j * HALF, HALF), HALF), :]
        part_send[j] = dot(cot[...], rows, 1, 1).astype(BF16)
    loads[5].wait()

    pl.semaphore_wait(barrier, SEQ)

    def across_copy(src, dst, sems, j):
        return pltpu.make_async_remote_copy(
            src, dst, sems.at[j], sems.at[2 + j], device_id=across, device_id_type=MESH
        )

    def to_peer(src, dst, send, recv, peer):
        return pltpu.make_async_remote_copy(
            src, dst, send, recv, device_id={"seq": peer}, device_id_type=MESH
        )

    def spread(send, recv, k, j):
        @pl.loop(1, CHIPS)
        def _(s):
            t = lax.rem(chip + s, CHIPS)
            to_peer(
                send.at[j * CHIPS + t], recv.at[me], send_sem.at[k], recv_sem.at[k], 2 * t + j
            ).start()

    def spread_near(send, recv, k):
        to_peer(
            send.at[(1 - core) * CHIPS + chip], recv.at[me], send_sem.at[k], recv_sem.at[k], partner
        ).start()
        pltpu.make_async_copy(send.at[hub], recv.at[me], recv_sem.at[k]).start()

    def give_back(send, recv, k, sems):
        @pl.loop(1, SEQ)
        def _(s):
            peer = lax.rem(me + s, SEQ)
            to_peer(send.at[peer], recv.at[hub], send_sem.at[k], sems.at[core], peer).start()

        pltpu.make_async_copy(send.at[me], recv.at[hub], sems.at[core]).start()

    def wait_all(ref, sem):
        pltpu.make_async_copy(ref, ref, sem).wait()

    def mix(recv, send, back):
        for k in range(COLS):
            lanes = pl.ds(k * 128, 128)
            wide[k] = recv[:, :, lanes].astype(F32).reshape(SEQ * ROWS, 128)
        for i in range(ROWS):
            at = pl.ds(i, SEQ, stride=ROWS)
            rows = [wide[k, at, :].astype(BF16) for k in range(COLS)]
            part = dot(second[i], jnp.concatenate(rows, axis=1), 0 if back else 1, 0)
            for k in range(COLS):
                wide_out[k, at, :] = part[:, k * 128 : (k + 1) * 128]
        for k in range(COLS):
            lanes = pl.ds(k * 128, 128)
            send[:, :, lanes] = wide_out[k].reshape(SEQ, ROWS, 128).astype(BF16)

    share = to_peer(
        second.at[pl.ds(core * 4, 4)],
        second.at[pl.ds(core * 4, 4)],
        second_sem.at[0],
        second_sem.at[1],
        partner,
    )
    share.start()
    parts = [across_copy(part_send.at[j], part_recv.at[j], part_sem, j) for j in range(2)]
    for copy in parts:
        copy.start()
    spread(a_send, a_recv, 0, 0)
    spread(a_send, a_recv, 0, 1)
    spread_near(a_send, a_recv, 0)

    loads[4].wait()
    for j in range(2):
        value = gate_in[:, columns(j)].astype(F32)
        gate[:, columns(j)] = value / (1.0 + jnp.exp(-value))
        rows = weight[pl.ds(pl.multiple_of(ch * WIDTH + j * HALF, HALF), HALF), :]
        own_part[:, columns(j)] = dot(cot[...], rows, 1, 1)

    for j in range(2):
        parts[j].wait_recv()
        grad_gated = (own_part[:, columns(j)] + part_recv[j].astype(F32)).astype(BF16)
        grad_mixed = grad_gated.astype(F32) * gate[:, columns(j)]
        b_send[slots(j)] = grad_mixed.reshape(CHIPS, ROWS, HALF).astype(BF16)
        spread(b_send, b_recv, 1, j)
    spread_near(b_send, b_recv, 1)

    share.wait_recv()
    wait_all(a_recv, recv_sem.at[0])
    mix(a_recv, m_send, False)
    give_back(m_send, a_ret, 2, a_ret_sem)

    wait_all(b_recv, recv_sem.at[1])
    mix(b_recv, g_send, True)
    give_back(g_send, b_ret, 3, b_ret_sem)

    gates = [across_copy(gated.at[j], gated_other.at[j], gated_sem, j) for j in range(2)]
    for j in range(2):
        wait_all(a_ret.at[slots(j)], a_ret_sem.at[j])
        mixed = a_ret[slots(j)].astype(F32).reshape(BLOCK, HALF)
        gated[j] = (mixed * gate[:, columns(j)]).astype(BF16)
        gates[j].start()
    for j in range(2):
        rows = weight[pl.ds(pl.multiple_of(ch * WIDTH + j * HALF, HALF), HALF), :]
        if j == 0:
            total[...] = dot(gated[j], rows)
        else:
            total[...] += dot(gated[j], rows)

    for j in range(2):
        wait_all(b_ret.at[slots(j)], b_ret_sem.at[j])
        grad_first = b_ret[slots(j)].astype(F32).reshape(BLOCK, HALF).astype(BF16)
        grad_ref[:, columns(j)] = dot(blocks[0], grad_first, 0, 0).astype(BF16)

    for j in range(2):
        gates[j].wait_recv()
        rows = weight[pl.ds(pl.multiple_of((1 - ch) * WIDTH + j * HALF, HALF), HALF), :]
        if j == 0:
            total[...] += dot(gated_other[j], rows)
        else:
            result_ref[...] = (total[...] + dot(gated_other[j], rows)).astype(BF16)

    for j in range(2):
        parts[j].wait_send()
        gates[j].wait_send()
    share.wait_send()
    for k, ref in enumerate((a_send, b_send, m_send, g_send)):
        sent = ref.at[pl.ds(0, SEQ - 1)]
        wait_all(sent, send_sem.at[k])


def body(seq_in, gate_in, first_blocks, second_blocks, out_weight, cotangent):
    whole = pltpu.VMEM((BLOCK, WIDTH), BF16)
    whole_f32 = pltpu.VMEM((BLOCK, WIDTH), F32)
    halves = pltpu.VMEM((2, BLOCK, HALF), BF16)
    messages = pltpu.VMEM((SEQ, ROWS, HALF), BF16)
    wide = pltpu.VMEM((COLS, SEQ * ROWS, 128), F32)
    dma = pltpu.SemaphoreType.DMA
    out = jax.ShapeDtypeStruct((BLOCK, WIDTH), BF16)
    return pl.pallas_call(
        kernel,
        out_shape=(out, out),
        in_specs=[pl.BlockSpec(memory_space=pl.ANY)] * 6,
        out_specs=(pl.BlockSpec(memory_space=pltpu.VMEM),) * 2,
        scratch_shapes=[
            whole,
            whole,
            pltpu.VMEM((1, BLOCK, BLOCK), BF16),
            pltpu.VMEM((ROWS, SEQ, SEQ), BF16),
            pltpu.VMEM((2 * WIDTH, WIDTH), BF16),
            whole,
            whole_f32,
            whole_f32,
            halves,
            halves,
        ]
        + [messages] * 8
        + [wide, wide, halves, halves, whole_f32]
        + [dma((6,)), dma((2,)), dma((4,)), dma((4,)), dma((4,)), dma((2,)), dma((2,)), dma((2,))],
        compiler_params=pltpu.CompilerParams(
            collective_id=0, has_side_effects=True, vmem_limit_bytes=62 * 2**20
        ),
        cost_estimate=pl.CostEstimate(
            flops=3_500_000_000, bytes_accessed=7_000_000, transcendentals=400_000
        ),
        name="monarch",
    )(seq_in, gate_in, first_blocks, second_blocks, out_weight, cotangent)


def solution(mesh):
    return jax.shard_map(
        body,
        mesh=mesh,
        in_specs=(
            P("seq", "ch"),
            P("seq", "ch"),
            P("seq", None, None),
            P("seq", None, None),
            P(None, "ch"),
            P("seq", "ch"),
        ),
        out_specs=(P("seq", "ch"), P("seq", "ch")),
        check_vma=False,
    )
```

profile of v0, /device:TPU:1, one launch (start us, length us, event | category | flops | bytes accessed | tf_op | source)
XLA Modules:
  0.0 103.4 jit_solution(13610329917941475902)
XLA Ops:
  0.6 98.7 %monarch.1 = (bf16[512,768]{1,0:T(8,128)(2,1)}, bf16[512,768]{1,0:T(8,128)(2,1)}) custom-call(bf16[512,768]{1,0:T(8,128)(2,1)} %seq_hbm.1, bf16[512,768]{1,0:T(8,128)(2,1)} %gate_hbm.1, bf16[1,512,512]{2,1,0:T(8,128)(2,1)} %first_hbm.1, bf16[4,128,128]{2,1,0:T(8,128)(2,1)} %second_hbm.1, bf16[1536,768]{1,0:T(8,128)(2,1)} %weight_hbm.1, bf16[512,768]{1,0:T(8,128)(2,1)} %cot_hbm.1), custom_call_target="tpu_custom_call" | custom-call | flops 3500000000 | bytes 7000000 | tf_op jit(solution)/shard_map/monarch/pallas_call | solution.py:218
  99.3 2.1 %copy.10 = bf16[512,768]{1,0:T(8,128)(2,1)} copy(bf16[512,768]{1,0:T(8,128)(2,1)} %get-tuple-element.4) | data formatting | bytes 1572864
  101.4 2.1 %copy.11 = bf16[512,768]{1,0:T(8,128)(2,1)} copy(bf16[512,768]{1,0:T(8,128)(2,1)} %get-tuple-element.5) | data formatting | bytes 1572864
where the time goes:
time: 104 us; the launch traced here: 103 us
  Pallas kernels  98.7 us (95%)
  local copies, waits for them, and re-layouts  4.13 us (4%)
    pallas_call x1, Pallas kernels, body(): pl.pallas_call(kernel, out_shape=(out, out), in_specs=[pl.BlockSpec(memor...  98.7 us
    unnamed x2, local copies, waits for them, and re-layouts  4.13 us

commit v1 on v0

--- a/solution.py
+++ b/solution.py
@@ -142,8 +142,7 @@
     )
     share.start()
     parts = [across_copy(part_send.at[j], part_recv.at[j], part_sem, j) for j in range(2)]
-    for copy in parts:
-        copy.start()
+    parts[0].start()
     spread(a_send, a_recv, 0, 0)
     spread(a_send, a_recv, 0, 1)
     spread_near(a_send, a_recv, 0)
@@ -155,18 +154,22 @@
         rows = weight[pl.ds(pl.multiple_of(ch * WIDTH + j * HALF, HALF), HALF), :]
         own_part[:, columns(j)] = dot(cot[...], rows, 1, 1)
 
-    for j in range(2):
+    def send_grad(j):
         parts[j].wait_recv()
+        if j == 0:
+            parts[1].start()
         grad_gated = (own_part[:, columns(j)] + part_recv[j].astype(F32)).astype(BF16)
         grad_mixed = grad_gated.astype(F32) * gate[:, columns(j)]
         b_send[slots(j)] = grad_mixed.reshape(CHIPS, ROWS, HALF).astype(BF16)
         spread(b_send, b_recv, 1, j)
-    spread_near(b_send, b_recv, 1)
-
+
+    send_grad(0)
     share.wait_recv()
     wait_all(a_recv, recv_sem.at[0])
     mix(a_recv, m_send, False)
     give_back(m_send, a_ret, 2, a_ret_sem)
+    send_grad(1)
+    spread_near(b_send, b_recv, 1)
 
     wait_all(b_recv, recv_sem.at[1])
     mix(b_recv, g_send, True)
@@ -214,7 +217,7 @@
     messages = pltpu.VMEM((SEQ, ROWS, HALF), BF16)
     wide = pltpu.VMEM((COLS, SEQ * ROWS, 128), F32)
     dma = pltpu.SemaphoreType.DMA
-    out = jax.ShapeDtypeStruct((BLOCK, WIDTH), BF16)
+    out = pltpu.VMEM((BLOCK, WIDTH), BF16)
     return pl.pallas_call(
         kernel,
         out_shape=(out, out),
@@ -236,7 +239,7 @@
         + [wide, wide, halves, halves, whole_f32]
         + [dma((6,)), dma((2,)), dma((4,)), dma((4,)), dma((4,)), dma((2,)), dma((2,)), dma((2,))],
         compiler_params=pltpu.CompilerParams(
-            collective_id=0, has_side_effects=True, vmem_limit_bytes=62 * 2**20
+            collective_id=0, has_side_effects=True, vmem_limit_bytes=60 * 2**20
         ),
         cost_estimate=pl.CostEstimate(
             flops=3_500_000_000, bytes_accessed=7_000_000, transcendentals=400_000

time: 104 us -> 91.9 us (0.88)
  Pallas kernels: 98.7 us -> 89.4 us
  local copies, waits for them, and re-layouts: 4.13 us -> 1.76 us
    pallas_call x1, Pallas kernels: 98.7 us -> 89.4 us  [body(): pl.pallas_call(kernel, out_shape=(out, out), in_specs=[pl.BlockSpec(memor...]
    unnamed x2, local copies, waits for them, and re-layouts: 4.13 us -> 1.76 us
where the time goes in v1:
time: 91.9 us
  Pallas kernels  89.4 us (97%)
  local copies, waits for them, and re-layouts  1.76 us (2%)
    pallas_call x1, Pallas kernels, body(): pl.pallas_call(kernel, out_shape=(out, out), in_specs=[pl.BlockSpec(memor...  89.4 us

profile of v1, /device:TPU:1, one launch (start us, length us, event | category | flops | bytes accessed | tf_op | source)
XLA Modules:
  0.0 91.9 jit_solution(7713551579482450106)
XLA Ops:
  0.6 89.4 %monarch.1 = (bf16[512,768]{1,0:T(8,128)(2,1)S(1)}, bf16[512,768]{1,0:T(8,128)(2,1)S(1)}) custom-call(bf16[512,768]{1,0:T(8,128)(2,1)} %seq_hbm.1, bf16[512,768]{1,0:T(8,128)(2,1)} %gate_hbm.1, bf16[1,512,512]{2,1,0:T(8,128)(2,1)} %first_hbm.1, bf16[4,128,128]{2,1,0:T(8,128)(2,1)} %second_hbm.1, bf16[1536,768]{1,0:T(8,128)(2,1)} %weight_hbm.1, ...), custom_call_target="tpu_custom_call" | custom-call | flops 3500000000 | bytes 7000000 | tf_op jit(solution)/shard_map/monarch/pallas_call | solution.py:221
  90.1 0.9 copy.10
  91.0 0.9 copy.11

commit v2 on v1

--- a/solution.py
+++ b/solution.py
@@ -28,7 +28,7 @@
     gate, own_part, part_send, part_recv,
     a_send, a_recv, m_send, a_ret,
     b_send, b_recv, g_send, b_ret,
-    wide, wide_out, gated, gated_other, total,
+    wide, wide_out, gated, gated_other, total, blocks_t,
     load_sem, second_sem, part_sem, gated_sem, send_sem, recv_sem, a_ret_sem, b_ret_sem,
 ):
     me = lax.axis_index("seq")
@@ -95,24 +95,32 @@
         )
 
     def spread(send, recv, k, j):
-        @pl.loop(1, CHIPS)
+        @pl.loop(1, CHIPS, unroll=7)
         def _(s):
             t = lax.rem(chip + s, CHIPS)
             to_peer(
                 send.at[j * CHIPS + t], recv.at[me], send_sem.at[k], recv_sem.at[k], 2 * t + j
             ).start()
 
-    def spread_near(send, recv, k):
-        to_peer(
-            send.at[(1 - core) * CHIPS + chip], recv.at[me], send_sem.at[k], recv_sem.at[k], partner
-        ).start()
-        pltpu.make_async_copy(send.at[hub], recv.at[me], recv_sem.at[k]).start()
+        slot = j * CHIPS + chip
+
+        @pl.when(core == j)
+        def _():
+            pltpu.make_async_copy(send.at[slot], recv.at[me], recv_sem.at[k]).start()
+
+        @pl.when(core != j)
+        def _():
+            to_peer(send.at[slot], recv.at[me], send_sem.at[k], recv_sem.at[k], partner).start()
 
     def give_back(send, recv, k, sems):
-        @pl.loop(1, SEQ)
+        @pl.loop(1, CHIPS, unroll=7)
         def _(s):
-            peer = lax.rem(me + s, SEQ)
-            to_peer(send.at[peer], recv.at[hub], send_sem.at[k], sems.at[core], peer).start()
+            t = lax.rem(chip + s, CHIPS)
+            for j in range(2):
+                peer = 2 * t + j
+                to_peer(send.at[peer], recv.at[hub], send_sem.at[k], sems.at[core], peer).start()
+
+        to_peer(send.at[partner], recv.at[hub], send_sem.at[k], sems.at[core], partner).start()
 
         pltpu.make_async_copy(send.at[me], recv.at[hub], sems.at[core]).start()
 
@@ -145,7 +153,6 @@
     parts[0].start()
     spread(a_send, a_recv, 0, 0)
     spread(a_send, a_recv, 0, 1)
-    spread_near(a_send, a_recv, 0)
 
     loads[4].wait()
     for j in range(2):
@@ -169,8 +176,8 @@
     mix(a_recv, m_send, False)
     give_back(m_send, a_ret, 2, a_ret_sem)
     send_grad(1)
-    spread_near(b_send, b_recv, 1)
-
+
+    blocks_t[...] = blocks[0].T
     wait_all(b_recv, recv_sem.at[1])
     mix(b_recv, g_send, True)
     give_back(g_send, b_ret, 3, b_ret_sem)
@@ -191,7 +198,7 @@
     for j in range(2):
         wait_all(b_ret.at[slots(j)], b_ret_sem.at[j])
         grad_first = b_ret[slots(j)].astype(F32).reshape(BLOCK, HALF).astype(BF16)
-        grad_ref[:, columns(j)] = dot(blocks[0], grad_first, 0, 0).astype(BF16)
+        grad_ref[:, columns(j)] = dot(blocks_t[...], grad_first).astype(BF16)
 
     for j in range(2):
         gates[j].wait_recv()
@@ -208,6 +215,17 @@
     for k, ref in enumerate((a_send, b_send, m_send, g_send)):
         sent = ref.at[pl.ds(0, SEQ - 1)]
         wait_all(sent, send_sem.at[k])
+
+
+def write_out(result, grad_in, result_hbm, grad_hbm, sems):
+    copies = [
+        pltpu.make_async_copy(result, result_hbm, sems.at[0]),
+        pltpu.make_async_copy(grad_in, grad_hbm, sems.at[1]),
+    ]
+    for copy in copies:
+        copy.start()
+    for copy in copies:
+        copy.wait()
 
 
 def body(seq_in, gate_in, first_blocks, second_blocks, out_weight, cotangent):
@@ -218,7 +236,8 @@
     wide = pltpu.VMEM((COLS, SEQ * ROWS, 128), F32)
     dma = pltpu.SemaphoreType.DMA
     out = pltpu.VMEM((BLOCK, WIDTH), BF16)
-    return pl.pallas_call(
+    final = jax.ShapeDtypeStruct((BLOCK, WIDTH), BF16)
+    result, grad_in = pl.pallas_call(
         kernel,
         out_shape=(out, out),
         in_specs=[pl.BlockSpec(memory_space=pl.ANY)] * 6,
@@ -236,7 +255,7 @@
             halves,
         ]
         + [messages] * 8
-        + [wide, wide, halves, halves, whole_f32]
+        + [wide, wide, halves, halves, whole_f32, pltpu.VMEM((BLOCK, BLOCK), BF16)]
         + [dma((6,)), dma((2,)), dma((4,)), dma((4,)), dma((4,)), dma((2,)), dma((2,)), dma((2,))],
         compiler_params=pltpu.CompilerParams(
             collective_id=0, has_side_effects=True, vmem_limit_bytes=60 * 2**20
@@ -246,6 +265,17 @@
         ),
         name="monarch",
     )(seq_in, gate_in, first_blocks, second_blocks, out_weight, cotangent)
+    return pl.pallas_call(
+        write_out,
+        out_shape=(final, final),
+        in_specs=[pl.BlockSpec(memory_space=pl.ANY)] * 2,
+        out_specs=(pl.BlockSpec(memory_space=pl.ANY),) * 2,
+        scratch_shapes=[dma((2,))],
+        name="write_out",
+    )(
+        pltpu.with_memory_space_constraint(result, pltpu.VMEM),
+        pltpu.with_memory_space_constraint(grad_in, pltpu.VMEM),
+    )
 
 
 def solution(mesh):

time: 91.9 us -> 91.2 us (level)
  local copies, waits for them, and re-layouts: 1.76 us -> 0 us
  Pallas kernels: 89.4 us -> 90.4 us
    unnamed x2 -> x0, local copies, waits for them, and re-layouts: 1.76 us -> none
    pallas_call x0 -> x1, Pallas kernels: none -> 1.16 us  [body(): pl.pallas_call(write_out, out_shape=(final, final), in_specs=[pl.BlockSpe...]
where the time goes in v2:
time: 91.2 us; the launch traced here: 91.1 us
  Pallas kernels  90.4 us (99%)
    pallas_call x1, Pallas kernels, body(): pl.pallas_call(kernel, out_shape=(out, out), in_specs=[pl.BlockSpec(memor...  89.3 us

profile of v2, /device:TPU:1, one launch (start us, length us, event | category | flops | bytes accessed | tf_op | source)
XLA Modules:
  0.0 91.1 jit_solution(7682540589179046738)
XLA Ops:
  0.6 89.3 %monarch.1 = (bf16[512,768]{1,0:T(8,128)(2,1)S(1)}, bf16[512,768]{1,0:T(8,128)(2,1)S(1)}) custom-call(bf16[512,768]{1,0:T(8,128)(2,1)} %seq_hbm.1, bf16[512,768]{1,0:T(8,128)(2,1)} %gate_hbm.1, bf16[1,512,512]{2,1,0:T(8,128)(2,1)} %first_hbm.1, bf16[4,128,128]{2,1,0:T(8,128)(2,1)} %second_hbm.1, bf16[1536,768]{1,0:T(8,128)(2,1)} %weight_hbm.1, ...), custom_call_target="tpu_custom_call" | custom-call | flops 3500000000 | bytes 7000000 | tf_op jit(solution)/shard_map/monarch/pallas_call | solution.py:240
  89.9 1.2 %write_out.1 = (bf16[512,768]{1,0:T(8,128)(2,1)}, bf16[512,768]{1,0:T(8,128)(2,1)}) custom-call(bf16[512,768]{1,0:T(8,128)(2,1)S(1)} %get-tuple-element.4.result, bf16[512,768]{1,0:T(8,128)(2,1)S(1)} %get-tuple-element.5.grad_in), custom_call_target="tpu_custom_call" | custom-call | tf_op jit(solution)/shard_map/write_out/pallas_call | solution.py:268

commit v3 on v2

--- a/solution.py
+++ b/solution.py
@@ -130,7 +130,7 @@
     def mix(recv, send, back):
         for k in range(COLS):
             lanes = pl.ds(k * 128, 128)
-            wide[k] = recv[:, :, lanes].astype(F32).reshape(SEQ * ROWS, 128)
+            wide[k, pl.ds(0, SEQ * ROWS)] = recv[:, :, lanes].astype(F32).reshape(SEQ * ROWS, 128)
         for i in range(ROWS):
             at = pl.ds(i, SEQ, stride=ROWS)
             rows = [wide[k, at, :].astype(BF16) for k in range(COLS)]
@@ -139,7 +139,7 @@
                 wide_out[k, at, :] = part[:, k * 128 : (k + 1) * 128]
         for k in range(COLS):
             lanes = pl.ds(k * 128, 128)
-            send[:, :, lanes] = wide_out[k].reshape(SEQ, ROWS, 128).astype(BF16)
+            send[:, :, lanes] = wide_out[k, pl.ds(0, SEQ * ROWS)].reshape(SEQ, ROWS, 128).astype(BF16)
 
     share = to_peer(
         second.at[pl.ds(core * 4, 4)],
@@ -233,7 +233,7 @@
     whole_f32 = pltpu.VMEM((BLOCK, WIDTH), F32)
     halves = pltpu.VMEM((2, BLOCK, HALF), BF16)
     messages = pltpu.VMEM((SEQ, ROWS, HALF), BF16)
-    wide = pltpu.VMEM((COLS, SEQ * ROWS, 128), F32)
+    wide = pltpu.VMEM((COLS, SEQ * ROWS + ROWS, 128), F32)
     dma = pltpu.SemaphoreType.DMA
     out = pltpu.VMEM((BLOCK, WIDTH), BF16)
     final = jax.ShapeDtypeStruct((BLOCK, WIDTH), BF16)

time: 91.2 us -> 91.2 us (level)
  no operation moved by 1% of the time
where the time goes in v3:
time: 91.2 us; the launch traced here: 91.1 us
  Pallas kernels  90.4 us (99%)
    pallas_call x1, Pallas kernels, body(): pl.pallas_call(kernel, out_shape=(out, out), in_specs=[pl.BlockSpec(memor...  89.3 us

profile of v3, /device:TPU:1, one launch (start us, length us, event | category | flops | bytes accessed | tf_op | source)
XLA Modules:
  0.0 91.1 jit_solution(14432492428400470827)
XLA Ops:
  0.6 89.3 %monarch.1 = (bf16[512,768]{1,0:T(8,128)(2,1)S(1)}, bf16[512,768]{1,0:T(8,128)(2,1)S(1)}) custom-call(bf16[512,768]{1,0:T(8,128)(2,1)} %seq_hbm.1, bf16[512,768]{1,0:T(8,128)(2,1)} %gate_hbm.1, bf16[1,512,512]{2,1,0:T(8,128)(2,1)} %first_hbm.1, bf16[4,128,128]{2,1,0:T(8,128)(2,1)} %second_hbm.1, bf16[1536,768]{1,0:T(8,128)(2,1)} %weight_hbm.1, ...), custom_call_target="tpu_custom_call" | custom-call | flops 3500000000 | bytes 7000000 | tf_op jit(solution)/shard_map/monarch/pallas_call | solution.py:240
  89.9 1.2 %write_out.1 = (bf16[512,768]{1,0:T(8,128)(2,1)}, bf16[512,768]{1,0:T(8,128)(2,1)}) custom-call(bf16[512,768]{1,0:T(8,128)(2,1)S(1)} %get-tuple-element.4.result, bf16[512,768]{1,0:T(8,128)(2,1)S(1)} %get-tuple-element.5.grad_in), custom_call_target="tpu_custom_call" | custom-call | tf_op jit(solution)/shard_map/write_out/pallas_call | solution.py:268

commit v4 on v3

--- a/solution.py
+++ b/solution.py
@@ -38,6 +38,19 @@
     across = {"ch": 1 - ch}
     hub = core * CHIPS + chip
 
+    barrier = pltpu.get_barrier_semaphore()
+
+    @pl.loop(1, SEQ - 1, unroll=6)
+    def _(s):
+        pl.semaphore_signal(
+            barrier, inc=1, device_id={"seq": lax.rem(me + s, SEQ)}, device_id_type=MESH
+        )
+
+    pl.semaphore_signal(
+        barrier, inc=1, device_id={"seq": lax.rem(me + SEQ - 1, SEQ)}, device_id_type=MESH
+    )
+    pl.semaphore_signal(barrier, inc=1, device_id=across, device_id_type=MESH)
+
     loads = [
         pltpu.make_async_copy(src, dst, load_sem.at[k])
         for k, (src, dst) in enumerate(
@@ -53,16 +66,6 @@
     ]
     for load in loads:
         load.start()
-
-    barrier = pltpu.get_barrier_semaphore()
-
-    @pl.loop(1, SEQ)
-    def _(s):
-        pl.semaphore_signal(
-            barrier, inc=1, device_id={"seq": lax.rem(me + s, SEQ)}, device_id_type=MESH
-        )
-
-    pl.semaphore_signal(barrier, inc=1, device_id=across, device_id_type=MESH)
 
     def columns(j):
         return pl.ds(j * HALF, HALF)

time: 91.2 us -> 91 us (level)
  no operation moved by 1% of the time
where the time goes in v4:
time: 91 us
  Pallas kernels  90.3 us (99%)
    pallas_call x1, Pallas kernels, body(): pl.pallas_call(kernel, out_shape=(out, out), in_specs=[pl.BlockSpec(memor...  89.2 us

profile of v4, /device:TPU:1, one launch (start us, length us, event | category | flops | bytes accessed | tf_op | source)
XLA Modules:
  0.0 91.0 jit_solution(11524075907363125044)
XLA Ops:
  0.6 89.2 %monarch.1 = (bf16[512,768]{1,0:T(8,128)(2,1)S(1)}, bf16[512,768]{1,0:T(8,128)(2,1)S(1)}) custom-call(bf16[512,768]{1,0:T(8,128)(2,1)} %seq_hbm.1, bf16[512,768]{1,0:T(8,128)(2,1)} %gate_hbm.1, bf16[1,512,512]{2,1,0:T(8,128)(2,1)} %first_hbm.1, bf16[4,128,128]{2,1,0:T(8,128)(2,1)} %second_hbm.1, bf16[1536,768]{1,0:T(8,128)(2,1)} %weight_hbm.1, ...), custom_call_target="tpu_custom_call" | custom-call | flops 3500000000 | bytes 7000000 | tf_op jit(solution)/shard_map/monarch/pallas_call | solution.py:243
  89.8 1.2 %write_out.1 = (bf16[512,768]{1,0:T(8,128)(2,1)}, bf16[512,768]{1,0:T(8,128)(2,1)}) custom-call(bf16[512,768]{1,0:T(8,128)(2,1)S(1)} %get-tuple-element.4.result, bf16[512,768]{1,0:T(8,128)(2,1)S(1)} %get-tuple-element.5.grad_in), custom_call_target="tpu_custom_call" | custom-call | tf_op jit(solution)/shard_map/write_out/pallas_call | solution.py:271
